TPU v7x, 512 devices: a whole 4x4x16 slice. The times are simulated.
512 devices in a mesh: attn: 32 (over z_lo, y), exp: 8 (over x, core), shard: 2 (over z_hi).
Axes of the slice: x: 4, y: 4, z: 16 (z_hi: 2, z_lo: 8; z = z_hi * 8 + z_lo), core: 2. Of those that a mesh axis runs over, the one named last changes fastest.
Arguments:
- tokens: bfloat16 [8192, 3584], P(('attn', 'shard'), 'exp'), may hold values from -6 to 6
- route_ids: int32 [8192, 1], P(('attn', 'shard')), may hold values from 0 to 31; in each aligned block of 128 rows (0 to 127, 128 to 255, ...) at most 8 rows name the same one
- gate_values: float32 [8192, 1], P(('attn', 'shard')), may hold values from 0.2 to 1
- slot_table: int32 [32], replicated, may hold values from 0 to 31, each once
- w_gate: bfloat16 [32, 3584, 1024], P('attn', 'shard', 'exp'), may hold values from -0.09375 to 0.09375
- w_up: bfloat16 [32, 3584, 1024], P('attn', 'shard', 'exp'), may hold values from -0.09375 to 0.09375
- w_down: bfloat16 [32, 1024, 3584], P('attn', 'exp', 'shard'), may hold values from -0.1875 to 0.1875
- cotangent: bfloat16 [8192, 3584], P(('attn', 'shard'), 'exp'), may hold values from -6 to 6
Outputs:
- mixed: bfloat16 [8192, 3584], P(('attn', 'shard'), 'exp')
- token_grads: bfloat16 [8192, 3584], P(('attn', 'shard'), 'exp')
- grad_gate: float32 [32, 3584, 1024], P('attn', 'shard', 'exp')
- grad_up: float32 [32, 3584, 1024], P('attn', 'shard', 'exp')
- grad_down: float32 [32, 1024, 3584], P('attn', 'exp', 'shard')
Inputs may be any that keep to these rules, and one draw needn't show every extreme that they name: `route_ids`: among the 128 tokens of one source group no expert is named more than 8 times, a bound that some block reaches. `slot_table`: each slot holds exactly one expert.
All inputs are finite; a program needn't handle non-finite values.
Results may differ from a plain program's by a relative error of at most 0.018.
Values may be sent and summed in bfloat16 or wider, within the bound.
A program may use at most 64 MiB of HBM per device.

v0:
```python
import jax
import jax.numpy as jnp
from jax import lax
from jax.sharding import PartitionSpec as P


def from_partner(value, axis, stride):
    mask = 2**stride
    pairs = [(source, source ^ mask) for source in range(lax.axis_size(axis))]
    return lax.ppermute(value, axis, pairs)


def shards(tokens, route_ids, gate_values, slot_table, w_gate, w_up, w_down, cotangent):
    slot_count = lax.axis_size("attn")
    tok_count = tokens.shape[0]
    features = tokens.shape[1]
    capacity = 2 * tok_count // slot_count
    row_count = slot_count * capacity
    experts = jnp.arange(slot_count, dtype=jnp.int32)
    slot_of = jnp.sum(jnp.where(route_ids == experts[None, :], slot_table[None, :], 0), axis=1)
    member = (slot_of[:, None] == experts[None, :]).astype(jnp.int32)
    ranks = jnp.sum((jnp.cumsum(member, axis=0) - member) * member, axis=1)
    target = slot_of * capacity + ranks
    places = (jnp.arange(row_count, dtype=jnp.int32)[:, None] == target[None, :]).astype(
        jnp.bfloat16
    )
    owner = lax.axis_index("shard")

    def to_slots(values):
        spread = jnp.dot(places, values, preferred_element_type=jnp.float32)
        return spread.astype(jnp.bfloat16).reshape(slot_count, capacity, features)

    def from_slots(arrived):
        flat = arrived.reshape(row_count, features)
        return lax.dot_general(
            places, flat, (((0,), (0,)), ((), ())), preferred_element_type=jnp.float32
        )

    gate_full, up_full, down_full = (
        lax.all_gather(w_gate, "shard", axis=1, tiled=True),
        lax.all_gather(w_up, "shard", axis=1, tiled=True),
        lax.all_gather(w_down, "shard", axis=2, tiled=True),
    )
    gate_full = gate_full[0]
    up_full = up_full[0]
    down_full = down_full[0]
    hid_width = gate_full.shape[1]
    weighted_cot = (gate_values * cotangent.astype(jnp.float32)).astype(jnp.bfloat16)
    x_rows = lax.all_to_all(to_slots(tokens), "attn", split_axis=0, concat_axis=0, tiled=True)
    x_rows = x_rows.reshape(row_count, features)
    x_whole = lax.all_gather(x_rows, "exp", axis=1, tiled=True)
    pre_gate = jnp.dot(x_whole, gate_full, preferred_element_type=jnp.float32)
    pre_up = jnp.dot(x_whole, up_full, preferred_element_type=jnp.float32)
    hidden = (jax.nn.silu(pre_gate) * pre_up).astype(jnp.bfloat16)
    out_sum = lax.psum_scatter(
        lax.dot_general(
            down_full, hidden, (((0,), (1,)), ((), ())), preferred_element_type=jnp.float32
        ).astype(jnp.bfloat16),
        "exp",
        scatter_dimension=0,
        tiled=True,
    ).astype(jnp.float32)
    out_rows = out_sum.T.astype(jnp.bfloat16).reshape(slot_count, capacity, features)
    results = lax.all_to_all(out_rows, "attn", split_axis=0, concat_axis=0, tiled=True)
    mixed = (gate_values * from_slots(results)).astype(jnp.bfloat16)
    dy_rows = lax.all_to_all(
        to_slots(weighted_cot), "attn", split_axis=0, concat_axis=0, tiled=True
    )
    dy_whole = lax.all_gather(dy_rows.reshape(row_count, features), "exp", axis=1, tiled=True)
    d_hidden = lax.dot_general(
        dy_whole, down_full, (((1,), (1,)), ((), ())), preferred_element_type=jnp.float32
    )
    grad_down = lax.dot_general(
        hidden, dy_whole, (((0,), (0,)), ((), ())), preferred_element_type=jnp.float32
    )
    sigma = jax.nn.sigmoid(pre_gate)
    d_gate = (d_hidden * pre_up * sigma * (1.0 + pre_gate * (1.0 - sigma))).astype(jnp.bfloat16)
    d_up = (d_hidden * pre_gate * sigma).astype(jnp.bfloat16)
    d_both = jnp.concatenate([d_gate, d_up], axis=1)
    grads_in = lax.dot_general(
        x_whole, d_both, (((0,), (0,)), ((), ())), preferred_element_type=jnp.float32
    )
    grad_gate = grads_in[:, :hid_width]
    grad_up = grads_in[:, hid_width:]
    both_parts = jnp.concatenate([gate_full, up_full], axis=1)
    in_sum = lax.psum_scatter(
        lax.dot_general(
            both_parts, d_both, (((1,), (1,)), ((), ())), preferred_element_type=jnp.float32
        ).astype(jnp.bfloat16),
        "exp",
        scatter_dimension=0,
        tiled=True,
    ).astype(jnp.float32)
    in_rows = in_sum.T.astype(jnp.bfloat16).reshape(slot_count, capacity, features)
    returned = lax.all_to_all(in_rows, "attn", split_axis=0, concat_axis=0, tiled=True)
    token_grads = from_slots(returned).astype(jnp.bfloat16)
    stacked = jnp.stack([grad_gate, grad_up, grad_down.T])
    half_rows = stacked.shape[1] // 2
    given = lax.dynamic_slice_in_dim(stacked, (1 - owner) * half_rows, half_rows, 1)
    kept = lax.dynamic_slice_in_dim(stacked, owner * half_rows, half_rows, 1)
    totals = kept + from_partner(given.astype(jnp.bfloat16), "shard", 0).astype(given.dtype)
    return (mixed, token_grads, totals[0][None], totals[1][None], totals[2].T[None])


def solution(mesh):
    in_specs = (
        P(("attn", "shard"), "exp"),
        P(("attn", "shard"), None),
        P(("attn", "shard"), None),
        P(),
        P("attn", "shard", "exp"),
        P("attn", "shard", "exp"),
        P("attn", "exp", "shard"),
        P(("attn", "shard"), "exp"),
    )
    out_specs = (
        P(("attn", "shard"), "exp"),
        P(("attn", "shard"), "exp"),
        P("attn", "shard", "exp"),
        P("attn", "shard", "exp"),
        P("attn", "exp", "shard"),
    )
    return jax.shard_map(shards, mesh=mesh, in_specs=in_specs, out_specs=out_specs, check_vma=False)
```

profile of v0, /device:TPU:1, one launch (start us, length us, event | category | flops | bytes accessed | tf_op | source)
XLA Modules:
  0.0 372.7 jit_solution(5054713264630961292)
XLA Ops:
  8.5 1.1 convolution_convert_fusion.2
  9.8 32.6 %all_to_all.20 = bf16[32,8,448]{2,1,0:T(8,128)(2,1)S(1)} all-to-all(bf16[32,8,448]{2,1,0:T(8,128)(2,1)S(1)} %bitcast.54), channel_id=1, replica_groups=mesh['attn'=32,'exp'=8,'shard'=2] {'attn'}, dimensions={0} | all-to-all | bytes 458752 | tf_op jit(solution)/shard_map/all_to_all | solution.py:66
  43.7 24.4 %all_to_all.21 = bf16[32,8,448]{2,1,0:T(8,128)(2,1)S(1)} all-to-all(bf16[32,8,448]{2,1,0:T(8,128)(2,1)S(1)} %bitcast.56), channel_id=1, replica_groups=mesh['attn'=32,'exp'=8,'shard'=2] {'attn'}, dimensions={0} | all-to-all | bytes 458752 | tf_op jit(solution)/shard_map/all_to_all | solution.py:49
  69.0 43.7 %all_gather.18 = bf16[1,128,3584]{2,1,0:T(8,128)(2,1)S(1)} all-gather(bf16[1,128,1792]{2,1,0:T(8,128)(2,1)S(1)} %copy-done.9), channel_id=1, replica_groups=mesh['attn'=32,'exp'=8,'shard'=2] {'shard'}, dimensions={2}, use_global_device_ids=true | all-gather | bytes 1376256 | tf_op jit(solution)/shard_map/all_gather | solution.py:42
  112.8 47.1 %all_gather.17 = bf16[1,3584,128]{2,1,0:T(8,128)(2,1)S(1)} all-gather(bf16[1,1792,128]{2,1,0:T(8,128)(2,1)S(1)} %copy-done.10), channel_id=1, replica_groups=mesh['attn'=32,'exp'=8,'shard'=2] {'shard'}, dimensions={1}, use_global_device_ids=true | all-gather | bytes 1376256 | tf_op jit(solution)/shard_map/all_gather | solution.py:41
  159.8 29.0 %all_gather.16 = bf16[1,3584,128]{2,1,0:T(8,128)(2,1)S(1)} all-gather(bf16[1,1792,128]{2,1,0:T(8,128)(2,1)S(1)} %copy-done.11), channel_id=1, replica_groups=mesh['attn'=32,'exp'=8,'shard'=2] {'shard'}, dimensions={1}, use_global_device_ids=true | all-gather | bytes 1376256 | tf_op jit(solution)/shard_map/all_gather | solution.py:40
  188.9 2.2 fusion.5
  191.2 2.1 fusion.19
  194.5 2.3 copy.24
  198.3 1.9 convolution_convert_fusion.1
  200.2 1.5 copy-done.2
  204.5 2.4 copy-done.1
  207.1 4.8 %collective-permute-start = (bf16[3,1792,128]{2,1,0:T(8,128)(2,1)S(1)}, bf16[3,1792,128]{2,1,0:T(8,128)(2,1)S(1)}, u32[]{:S(2)}, u32[]{:S(2)}) collective-permute-start(bf16[3,1792,128]{2,1,0:T(8,128)(2,1)S(1)} %dynamic-slice_convert_fusion), channel_id=1, source_target_pairs={{0,1},{1,0},{2,3},{3,2},{4,5},{5,4},{6,7},{7,6},{8,9},{9,8},{10,11... | collective-permute-start | bytes 4128776 | tf_op jit(solution)/shard_map/ppermute | solution.py:10
  211.8 66.8 %reduce-scatter.7.cloned.1.call-done = bf16[448,256]{1,0:T(8,128)(2,1)} async-done(((bf16[3584,256]{1,0:T(8,128)(2,1)}), bf16[448,256]{1,0:T(8,128)(2,1)}) %reduce-scatter.7.cloned.1.call-update) | async-done | bytes 229392
  278.7 1.8 copy.25
  280.5 11.6 %all-to-all-start.1 = ((bf16[32,8,448]{2,1,0:T(8,128)(2,1)}), bf16[32,8,448]{2,1,0:T(8,128)(2,1)S(1)}, u32[]{:S(2)}, u32[]{:S(2)}) async-start(bf16[32,8,448]{2,1,0:T(8,128)(2,1)} %bitcast.9), calls=%async_computation.1 | async-start | bytes 524288 | tf_op jit(solution)/shard_map/all_to_all | solution.py:64
  292.1 29.1 %reduce-scatter.5.cloned.1.call-done = bf16[448,256]{1,0:T(8,128)(2,1)} async-done(((bf16[3584,256]{1,0:T(8,128)(2,1)}), bf16[448,256]{1,0:T(8,128)(2,1)}) %reduce-scatter.5.cloned.1.call-update) | async-done | bytes 229392 | tf_op jit(solution)/shard_map/reduce_scatter | solution.py:86
  321.2 1.8 copy.22
  322.9 19.9 %all-to-all-done.1 = bf16[32,8,448]{2,1,0:T(8,128)(2,1)S(1)} async-done(((bf16[32,8,448]{2,1,0:T(8,128)(2,1)}), bf16[32,8,448]{2,1,0:T(8,128)(2,1)S(1)}, u32[]{:S(2)}, u32[]{:S(2)}) %all-to-all-start.1) | async-done | bytes 229408 | tf_op jit(solution)/shard_map/all_to_all | solution.py:64
  342.9 5.7 %all-to-all-start.3 = ((bf16[32,8,448]{2,1,0:T(8,128)(2,1)}), bf16[32,8,448]{2,1,0:T(8,128)(2,1)S(1)}, u32[]{:S(2)}, u32[]{:S(2)}) async-start(bf16[32,8,448]{2,1,0:T(8,128)(2,1)} %bitcast.53), calls=%async_computation.4 | async-start | bytes 524288 | tf_op jit(solution)/shard_map/all_to_all | solution.py:95
  348.6 2.0 convert_add_fusion
  350.6 1.4 slice_bitcast_fusion.2
  352.0 1.2 copy.23
  354.1 11.1 %all-to-all-done.3 = bf16[32,8,448]{2,1,0:T(8,128)(2,1)S(1)} async-done(((bf16[32,8,448]{2,1,0:T(8,128)(2,1)}), bf16[32,8,448]{2,1,0:T(8,128)(2,1)S(1)}, u32[]{:S(2)}, u32[]{:S(2)}) %all-to-all-start.3) | async-done | bytes 229408 | tf_op jit(solution)/shard_map/all_to_all | solution.py:95
  (54 shorter events, 11.1 us)
Async XLA Ops:
  7.2 36.2 %copy-start = (bf16[128,448]{0,1:T(8,128)(2,1)S(1)}, bf16[128,448]{0,1:T(8,128)(2,1)}, u32[]{:S(2)}) copy-start(bf16[128,448]{0,1:T(8,128)(2,1)} %param.8) | copy-start | bytes 344068
  7.2 181.7 %all-gather.5.cloned.1.call-start = ((), (), s32[]{:S(2)}) async-start(), calls=%async_computation.7 | async-start | bytes 2064384 | tf_op jit(solution)/shard_map/all_gather | solution.py:69
  9.7 59.4 %copy-start.9 = (bf16[1,128,1792]{2,1,0:T(8,128)(2,1)S(1)}, bf16[1,128,1792]{2,1,0:T(8,128)(2,1)}, u32[]{:S(2)}) copy-start(bf16[1,128,1792]{2,1,0:T(8,128)(2,1)} %param.14) | copy-start | bytes 1376260
  43.3 69.5 %copy-start.10 = (bf16[1,1792,128]{2,1,0:T(8,128)(2,1)S(1)}, bf16[1,1792,128]{2,1,0:T(8,128)(2,1)}, u32[]{:S(2)}) copy-start(bf16[1,1792,128]{2,1,0:T(8,128)(2,1)} %param.13) | copy-start | bytes 1376260
  43.3 147.8 %all-gather.3.cloned.1.call-start = ((), (), s32[]{:S(2)}) async-start(), calls=%async_computation.6 | async-start | bytes 2064384 | tf_op jit(solution)/shard_map/all_gather | solution.py:51
  68.1 91.7 %copy-start.11 = (bf16[1,1792,128]{2,1,0:T(8,128)(2,1)S(1)}, bf16[1,1792,128]{2,1,0:T(8,128)(2,1)}, u32[]{:S(2)}) copy-start(bf16[1,1792,128]{2,1,0:T(8,128)(2,1)} %param.12) | copy-start | bytes 1376260
  69.0 209.7 %reduce-scatter.7.cloned.1.call-start = ((), (), s32[]{:S(2)}) async-start(), calls=%async_computation.9 | async-start | bytes 2064384
  159.8 31.3 %copy-start.5 = (bf16[1,3584,128]{2,1,0:T(8,128)(2,1)}, bf16[1,3584,128]{2,1,0:T(8,128)(2,1)S(1)}, u32[]{:S(2)}) copy-start(bf16[1,3584,128]{2,1,0:T(8,128)(2,1)S(1)} %all_gather.17) | copy-start | bytes 2752516
  188.9 4.5 %copy-start.7 = (bf16[1,3584,128]{2,1,0:T(8,128)(2,1)}, bf16[1,3584,128]{2,1,0:T(8,128)(2,1)S(1)}, u32[]{:S(2)}) copy-start(bf16[1,3584,128]{2,1,0:T(8,128)(2,1)S(1)} %all_gather.16) | copy-start | bytes 2752516
  191.1 2.2 copy-start.3
  196.8 1.2 copy-start.6
  196.8 1.5 copy-start.8
  196.8 124.3 %reduce-scatter.5.cloned.1.call-start = ((), (), s32[]{:S(2)}) async-start(), calls=%async_computation.8 | async-start | bytes 2064384 | tf_op jit(solution)/shard_map/reduce_scatter | solution.py:86
  200.2 1.5 copy-start.2
  201.7 1.5 copy-start.4
  204.5 2.4 copy-start.1
  207.1 141.5 %collective-permute-start = (bf16[3,1792,128]{2,1,0:T(8,128)(2,1)S(1)}, bf16[3,1792,128]{2,1,0:T(8,128)(2,1)S(1)}, u32[]{:S(2)}, u32[]{:S(2)}) collective-permute-start(bf16[3,1792,128]{2,1,0:T(8,128)(2,1)S(1)} %dynamic-slice_convert_fusion), channel_id=1, source_target_pairs={{0,1},{1,0},{2,3},{3,2},{4,5},{5,4},{6,7},{7,6},{8,9},{9,8},{10,11... | collective-permute-start | bytes 4128776 | tf_op jit(solution)/shard_map/ppermute | solution.py:10
  280.5 62.4 %all-to-all-start.1 = ((bf16[32,8,448]{2,1,0:T(8,128)(2,1)}), bf16[32,8,448]{2,1,0:T(8,128)(2,1)S(1)}, u32[]{:S(2)}, u32[]{:S(2)}) async-start(bf16[32,8,448]{2,1,0:T(8,128)(2,1)} %bitcast.9), calls=%async_computation.1 | async-start | bytes 524288 | tf_op jit(solution)/shard_map/all_to_all | solution.py:64
  342.9 22.4 %all-to-all-start.3 = ((bf16[32,8,448]{2,1,0:T(8,128)(2,1)}), bf16[32,8,448]{2,1,0:T(8,128)(2,1)S(1)}, u32[]{:S(2)}, u32[]{:S(2)}) async-start(bf16[32,8,448]{2,1,0:T(8,128)(2,1)} %bitcast.53), calls=%async_computation.4 | async-start | bytes 524288 | tf_op jit(solution)/shard_map/all_to_all | solution.py:95
  352.0 1.2 copy-start.12
Sparse Core Ops, SparseCore 0:
  43.4 30.3 all-gather.4
  76.0 32.7 all-gather.2
  197.0 81.6 reduce-scatter.6
  281.4 39.7 reduce-scatter.4
where the time goes:
time: 378 us; the launch traced here: 373 us
  blocking collectives  177 us (47%)
  waiting for transfers between devices  127 us (34%)
  starting transfers between devices  22.2 us (6%)
  local copies, waits for them, and re-layouts  17 us (4%)
  between operations  14 us (4%)
  matrix products  12 us (3%)
    unnamed x5, waiting for transfers between devices  66.9 us
    all_gather x1, blocking collectives, shards(): lax.all_gather(w_up, 'shard', axis=1, tiled=True)  47.1 us
    all_gather x1, blocking collectives, shards(): lax.all_gather(w_down, 'shard', axis=2, tiled=True)  43.7 us
    all_to_all x1, blocking collectives, shards(): lax.all_to_all(to_slots(weighted_cot), 'attn', split_axis=0, concat_axis=...  32.6 us
    reduce_scatter x1, waiting for transfers between devices, shards(): lax.psum_scatter(lax.dot_general(both_parts, d_both, (((1,), (1,)), ((),...  29.1 us
    all_gather x1, blocking collectives, shards(): lax.all_gather(w_gate, 'shard', axis=1, tiled=True)  29 us
    all_to_all x1, blocking collectives, shards(): lax.all_to_all(to_slots(tokens), 'attn', split_axis=0, concat_axis=0, til...  24.4 us
    all_to_all x1, waiting for transfers between devices, shards(): lax.all_to_all(out_rows, 'attn', split_axis=0, concat_axis=0, tiled=True)  19.9 us
  transfers between devices with their start and end apart: 7, of which 4 were waited for; matrix products, arithmetic and copies ran while one was open for 4% of the time, Pallas kernels for 0%

commit v1 on v0

v1 whole, which is shorter than its diff:
```python
import functools

import jax
import jax.numpy as jnp
from jax import lax
from jax.experimental import pallas as pl
from jax.experimental.pallas import tpu as pltpu
from jax.sharding import PartitionSpec as P

CHUNKS = 4
WIDE = 896
HALF = 448
WINDOW = 512
F32 = jnp.float32
BF16 = jnp.bfloat16


def base_offset(chunk, pair):
    first = jnp.where(chunk == 0, 0, chunk)
    second = jnp.where(chunk == 0, 4, 8 - chunk)
    return jnp.where(pair == 0, first, second)


def place():
    a, e, s = lax.axis_index("attn"), lax.axis_index("exp"), lax.axis_index("shard")
    return a % 4, a // 4 + 8 * s, e // 2, e % 2, s


def device(y, z, x, c):
    return {"attn": (z % 8) * 4 + y, "exp": 2 * x + c, "shard": z // 8}


def send(src, dst, send_sem, recv_sem, target):
    return pltpu.make_async_remote_copy(
        src_ref=src,
        dst_ref=dst,
        send_sem=send_sem,
        recv_sem=recv_sem,
        device_id=target,
        device_id_type=pl.DeviceIdType.MESH,
    )


def wait_for(ref, sem):
    pltpu.make_async_copy(ref, ref, sem).wait()


def last_last(a, b):
    return lax.dot_general(a, b, (((1,), (1,)), ((), ())), preferred_element_type=F32)


def first_first(a, b):
    return lax.dot_general(a, b, (((0,), (0,)), ((), ())), preferred_element_type=F32)


def dot(a, b):
    return jnp.dot(a, b, preferred_element_type=F32)


def kernel(
    xs, pp, wg, wu, wd, fin, gg, gu, gd,
    tok, sb, rows, wgu, acc, es, er, lg, os, orr, cs, xr, rb, rr, tb, tr,
    tok_s, tok_r, d_s, d_r, ag_s, ag_r, sf_s, sf_r, e_s, e_r, o_s, o_r, x_s, x_r, b_s, b_r, t_s, t_r,
):
    y, z, x, c, s = place()
    other = 3 - x
    p_own = jnp.where(x // 2 == s, 0, 1)
    qi_own = jnp.where(p_own == 0, x, other) - 2 * s
    h_src = jnp.where(c == 0, x, other) // 2
    h_fin = x // 2
    x_fin = jnp.where(p_own == 0, x, other)
    has_self = (c == 0) & (p_own == 0)
    sibling = device(y, z, x, 1 - c)
    partner = device(y, (z + 8) % 16, x, c)

    def piece_of(xx):
        p = jnp.where(xx // 2 == s, 0, 1)
        return jnp.where(p == 0, xx, 3 - xx) - 2 * s, p

    barrier = pltpu.get_barrier_semaphore()

    def greet(target):
        pl.semaphore_signal(barrier, inc=1, device_id=target, device_id_type=pl.DeviceIdType.MESH)

    greet(sibling)
    greet(partner)
    for r in (1, 2, 3):
        greet(device(y, z, (x + r) % 4, c))

    @pl.when(c == 0)
    def _():
        greet(device(y, z, x, 1))

    @pl.when(c == 1)
    def _():
        greet(device(y, z, other, 0))
        greet(device(y, z, other, 1))

    def greet_sources(i, carry):
        @pl.when(jnp.logical_not(has_self & (i == 0)))
        def _():
            greet(device((y + p_own + 2 * c) % 4, (z + i) % 16, x, p_own))

        return carry

    lax.fori_loop(0, 16, greet_sources, 0)
    x_back = jnp.where(c == 0, x, other)

    def greet_owners(i, carry):
        c_r = i % 2
        zz = 8 * h_fin + i // 2

        @pl.when(jnp.logical_not(has_self & (c_r == 0) & (zz == z)))
        def _():
            greet(device((y + 8 - c - 2 * c_r) % 4, zz, x_back, c_r))

        return carry

    lax.fori_loop(0, 16, greet_owners, 0)

    for q in range(2):
        wgu[q, :, 0:128] = wg[q * WIDE : (q + 1) * WIDE, :]
        wgu[q, :, 128:256] = wu[q * WIDE : (q + 1) * WIDE, :]

    pl.semaphore_wait(barrier, 5 + 1 + c + 32 - 2 * has_self.astype(jnp.int32))

    @pl.when(c == 0)
    def _():
        pltpu.make_async_copy(xs, tok.at[0], tok_r.at[0]).start()
        send(xs, tok.at[0], tok_s.at[0], tok_r.at[0], device(y, z, other, 1)).start()

    @pl.when(c == 1)
    def _():
        send(xs, tok.at[1], tok_s.at[0], tok_r.at[1], device(y, z, other, 1)).start()
        send(xs, tok.at[1], tok_s.at[1], tok_r.at[1], device(y, z, x, 0)).start()

    wait_for(tok.at[0], tok_r.at[0])
    wait_for(tok.at[1], tok_r.at[1])
    places = pp[...]
    left, right = tok[0], tok[1]
    whole = jnp.concatenate([left[:, :384], left[:, 384:] + right[:, :128], right[:, 128:]], axis=1)
    sb[...] = dot(places, whole).astype(BF16).reshape(16, 16, WIDE)

    def dispatch(i, carry):
        k, j, c_r = i // 4, (i // 2) % 2, i % 2
        zd = (z + 16 - base_offset(k, j)) % 16
        hi = jnp.where(zd // 8 == h_src, 0, 1)
        target = device((y + 8 - c - 2 * c_r) % 4, 8 * h_src + zd % 8, x, c_r)
        q_t = jnp.where(c == 0, x, other)
        there = rows.at[q_t - 2 * h_src, k, c_r, c, 2 * j + hi]
        mine = has_self & (i == 0)

        @pl.when(mine)
        def _():
            pltpu.make_async_copy(sb.at[i], there, d_r.at[k]).start()

        @pl.when(jnp.logical_not(mine))
        def _():
            send(sb.at[i], there, d_s.at[jnp.where(i == 0, CHUNKS, k)], d_r.at[k], target).start()

        return carry

    lax.fori_loop(0, 16, dispatch, 0)

    def gather(k):
        own = rows.at[qi_own, k, c, p_own]
        wait_for(own, d_r.at[k])
        for r in (1, 2, 3):
            send(own, own, ag_s.at[k, r - 1], ag_r.at[k, r - 1], device(y, z, (x + r) % 4, c)).start()

    def forward(k):
        for r in (1, 2, 3):
            qi, p = piece_of((x + 4 - r) % 4)
            wait_for(rows.at[qi, k, c, p], ag_r.at[k, r - 1])
        for q in range(2):
            send(rows.at[q, k, c], rows.at[q, k, c], sf_s.at[k, q], sf_r.at[k, q], sibling).start()

    def project(k):
        for q in range(2):
            wait_for(rows.at[q, k, 1 - c], sf_r.at[k, q])
        both = jnp.zeros((256, 256), F32)
        down = jnp.zeros((256, 128), F32)
        for q in range(2):
            block = rows[q, k].reshape(256, WIDE)
            both = both + dot(block, wgu[q])
            down = down + last_last(block, wd[:, q * WIDE : (q + 1) * WIDE])
        part = jnp.concatenate(
            [both.reshape(16, 2, 8, 256)[:, 0], down.reshape(16, 2, 8, 128)[:, 1]], axis=-1
        )
        acc[k] = part.reshape(128, 384)
        pairs = part.reshape(8, 2, 8, 384)
        es[k] = jnp.concatenate([pairs[:, 1:], pairs[:, :1]], axis=1).reshape(128, 384).astype(BF16)
        send(es.at[k], er.at[k], e_s.at[k], e_r.at[k], partner).start()

    def expand(k):
        wait_for(er.at[k], e_r.at[k])
        total = acc[k] + er[k].astype(F32)
        gate, up, d_hid = total[:, :128], total[:, 128:256], total[:, 256:]
        sigma = jax.nn.sigmoid(gate)
        hidden = gate * sigma * up
        d_gate = d_hid * up * sigma * (1.0 + gate * (1.0 - sigma))
        d_up = d_hid * gate * sigma
        d_both = jnp.concatenate([d_gate, d_up], axis=1)
        nothing = jnp.zeros((16, 8, 128), F32)
        top = jnp.concatenate([d_both.reshape(16, 8, 256), nothing], axis=-1)
        low = jnp.concatenate([nothing, nothing, hidden.reshape(16, 8, 128)], axis=-1)
        lg[k] = jnp.stack([top, low], axis=1).reshape(256, 384).astype(BF16)
        hidden, d_both = hidden.astype(BF16), d_both.astype(BF16)
        for q in range(2):
            outs = dot(hidden, wd[:, q * WIDE : (q + 1) * WIDE]).reshape(16, 8, WIDE)
            ins = last_last(d_both, wgu[q]).reshape(16, 8, WIDE)
            mixed = jnp.stack([outs, ins], axis=1).reshape(2, 2, 4, 16, WIDE).astype(BF16)
            os[k, 0, q] = mixed[0]
            os[k, 1, q] = mixed[1]
        send(os.at[k, 1 - c], orr.at[k], o_s.at[k], o_r.at[k], sibling).start()

    def scatter(k):
        wait_for(orr.at[k], o_r.at[k])
        for q in range(2):
            cs[k, q] = (os[k, c, q].astype(F32) + orr[k, q].astype(F32)).astype(BF16)
        for r in (1, 2, 3):
            xx = (x + r) % 4
            qi, p = piece_of(xx)
            send(cs.at[k, qi, p], xr.at[k, r - 1], x_s.at[k, r - 1], x_r.at[k, r - 1], device(y, z, xx, c)).start()

    def give_back(k):
        for r in (1, 2, 3):
            wait_for(xr.at[k, r - 1], x_r.at[k, r - 1])
        total = cs[k, qi_own, p_own].astype(F32)
        for r in range(3):
            total = total + xr[k, r].astype(F32)
        rb[k] = total.astype(BF16)
        for j in range(2):
            for hi in range(2):
                zs = (z + base_offset(k, j) + 8 * hi) % 16
                target = device((y + p_own + 2 * c) % 4, zs, x_fin, p_own)
                there = rr.at[4 * k + 2 * j + c]
                first = (j == 0) and (hi == 0)
                mine = has_self & (k == 0) if first else None
                sem = b_s.at[k, 2 * j + hi]
                if first:

                    @pl.when(mine)
                    def _():
                        pltpu.make_async_copy(rb.at[k, 0], there, b_r.at[k]).start()

                    @pl.when(jnp.logical_not(mine))
                    def _():
                        send(rb.at[k, 0], there, sem, b_r.at[k], target).start()

                else:
                    send(rb.at[k, 2 * j + hi], there, sem, b_r.at[k], target).start()

    stages = ((gather, 0), (forward, 1), (project, 2), (expand, 6), (scatter, 7), (give_back, 8))

    def step(t, carry):
        for stage, lag in stages:

            @pl.when((t >= lag) & (t < lag + CHUNKS))
            def _():
                stage(t - lag)

        return carry

    lax.fori_loop(0, CHUNKS + 8, step, 0)

    factors = lg[...].reshape(1024, 384).T
    for q in range(2):

        def columns(n, carry):
            lanes = pl.ds(pl.multiple_of(n * 128, 128), 128)
            block = rows[q, :, :, :, :, :, lanes].reshape(1024, 128)
            grads = dot(factors, block)
            at = pl.ds(pl.multiple_of(q * WIDE + n * 128, 128), 128)
            gg[at, :] = grads[:128].T
            gu[at, :] = grads[128:256].T
            gd[:, at] = grads[256:]
            return carry

        lax.fori_loop(0, 7, columns, 0)

    for k in range(CHUNKS):
        wait_for(rr.at[pl.ds(4 * k, 4)], b_r.at[k])
    tb[...] = first_first(places, rr[...].reshape(256, WIDE)).astype(BF16)
    theirs = pl.ds(pl.multiple_of(384 * (1 - c), 128), WINDOW)
    ours = pl.ds(pl.multiple_of(384 * c, 128), WINDOW)
    swap = send(tb.at[:, theirs], tr, t_s, t_r, sibling)
    swap.start()

    wait_for(xs, tok_s.at[0])

    @pl.when(c == 1)
    def _():
        wait_for(xs, tok_s.at[1])

    wait_for(sb.at[pl.ds(1, 3)], d_s.at[0])
    for k in range(1, CHUNKS):
        wait_for(sb.at[pl.ds(4 * k, 4)], d_s.at[k])

    @pl.when(jnp.logical_not(has_self))
    def _():
        wait_for(sb.at[0], d_s.at[CHUNKS])
        wait_for(rb.at[0, 0], b_s.at[0, 0])

    def drain(k, carry):
        for r in range(3):
            wait_for(xr.at[k, r], ag_s.at[k, r])
            wait_for(xr.at[k, r], x_s.at[k, r])
        for q in range(2):
            wait_for(rows.at[q, k, c], sf_s.at[k, q])
        wait_for(es.at[k], e_s.at[k])
        wait_for(orr.at[k], o_s.at[k])
        for i in range(4):
            if i == 0:

                @pl.when(k > 0)
                def _():
                    wait_for(rb.at[k, 0], b_s.at[k, 0])

            else:
                wait_for(rb.at[k, i], b_s.at[k, i])
        return carry

    lax.fori_loop(0, CHUNKS, drain, 0)
    swap.wait()
    fin[...] = tb[:, ours] + tr[...]


def shards(tokens, route_ids, gate_values, slot_table, w_gate, w_up, w_down, cotangent):
    y, z, x, c, _ = place()
    experts = jnp.arange(32, dtype=jnp.int32)
    slot_of = jnp.sum(jnp.where(route_ids == experts[None, :], slot_table[None, :], 0), axis=1)
    member = (slot_of[:, None] == experts[None, :]).astype(jnp.int32)
    ranks = jnp.sum((jnp.cumsum(member, axis=0) - member) * member, axis=1)

    index = jnp.arange(256, dtype=jnp.int32)
    block, kind, rank = index // 16, (index // 8) % 2, index % 8
    chunk, pair, core = block // 4, (block // 2) % 2, block % 2
    slot = ((z + 16 - base_offset(chunk, pair)) % 8) * 4 + (y + 8 - c - 2 * core) % 4
    hit = (slot[:, None] == slot_of[None, :]) & (rank[:, None] == ranks[None, :])
    hit = jnp.stack([hit & (kind == 0)[:, None], hit & (kind == 1)[:, None]], axis=1)
    places = hit.reshape(256, 256).astype(BF16)

    weighted = (gate_values * cotangent.astype(F32)).astype(BF16)
    stacked = jnp.concatenate([tokens, weighted], axis=0)
    stacked = jnp.where(
        c == 0, jnp.pad(stacked, ((0, 0), (0, 64))), jnp.pad(stacked, ((0, 0), (64, 0)))
    )
    vmem = pl.BlockSpec(memory_space=pltpu.VMEM)
    sem = pltpu.SemaphoreType.DMA
    fin, grad_gate, grad_up, grad_down = pl.pallas_call(
        kernel,
        name="expert_layer",
        out_shape=(
            jax.ShapeDtypeStruct((256, WINDOW), BF16),
            jax.ShapeDtypeStruct((1792, 128), F32),
            jax.ShapeDtypeStruct((1792, 128), F32),
            jax.ShapeDtypeStruct((128, 1792), F32),
        ),
        in_specs=[vmem] * 5,
        out_specs=(vmem,) * 4,
        scratch_shapes=[
            pltpu.VMEM((2, 256, WINDOW), BF16),
            pltpu.VMEM((16, 16, WIDE), BF16),
            pltpu.VMEM((2, CHUNKS, 2, 2, 4, 16, WIDE), BF16),
            pltpu.VMEM((2, WIDE, 256), BF16),
            pltpu.VMEM((CHUNKS, 128, 384), F32),
            pltpu.VMEM((CHUNKS, 128, 384), BF16),
            pltpu.VMEM((CHUNKS, 128, 384), BF16),
            pltpu.VMEM((CHUNKS, 256, 384), BF16),
            pltpu.VMEM((CHUNKS, 2, 2, 2, 4, 16, WIDE), BF16),
            pltpu.VMEM((CHUNKS, 2, 2, 4, 16, WIDE), BF16),
            pltpu.VMEM((CHUNKS, 2, 2, 4, 16, WIDE), BF16),
            pltpu.VMEM((CHUNKS, 3, 4, 16, WIDE), BF16),
            pltpu.VMEM((CHUNKS, 4, 16, WIDE), BF16),
            pltpu.VMEM((16, 16, WIDE), BF16),
            pltpu.VMEM((256, WIDE), BF16),
            pltpu.VMEM((256, WINDOW), BF16),
            sem((2,)),
            sem((2,)),
            sem((CHUNKS + 1,)),
            sem((CHUNKS,)),
            sem((CHUNKS, 3)),
            sem((CHUNKS, 3)),
            sem((CHUNKS, 2)),
            sem((CHUNKS, 2)),
            sem((CHUNKS,)),
            sem((CHUNKS,)),
            sem((CHUNKS,)),
            sem((CHUNKS,)),
            sem((CHUNKS, 3)),
            sem((CHUNKS, 3)),
            sem((CHUNKS, 4)),
            sem((CHUNKS,)),
            sem,
            sem,
        ],
        compiler_params=pltpu.CompilerParams(
            collective_id=0, has_side_effects=True, vmem_limit_bytes=48 * 2**20
        ),
    )(stacked, places, w_gate[0], w_up[0], w_down[0])
    fin = jnp.where(c == 0, fin[:, :HALF], fin[:, 64:])
    mixed = (gate_values * fin[:128].astype(F32)).astype(BF16)
    return mixed, fin[128:], grad_gate[None], grad_up[None], grad_down[None]


def solution(mesh):
    in_specs = (
        P(("attn", "shard"), "exp"),
        P(("attn", "shard"), None),
        P(("attn", "shard"), None),
        P(),
        P("attn", "shard", "exp"),
        P("attn", "shard", "exp"),
        P("attn", "exp", "shard"),
        P(("attn", "shard"), "exp"),
    )
    out_specs = (
        P(("attn", "shard"), "exp"),
        P(("attn", "shard"), "exp"),
        P("attn", "shard", "exp"),
        P("attn", "shard", "exp"),
        P("attn", "exp", "shard"),
    )
    return jax.shard_map(shards, mesh=mesh, in_specs=in_specs, out_specs=out_specs, check_vma=False)
```

time: 378 us -> 134 us (0.35)
  the two profiles are of different devices: /device:TPU:1 before, /device:TPU:33 now
where the time goes in v1:
time: 134 us
  Pallas kernels  122 us (91%)
  local copies, waits for them, and re-layouts  9.57 us (7%)
  other arithmetic  1.34 us (1%)
    pallas_call x1, Pallas kernels, shards(): pl.pallas_call(kernel, name='expert_layer', out_shape=(jax.ShapeDtypeStru...  122 us
    unnamed x21, local copies, waits for them, and re-layouts  9.56 us

profile of v1, /device:TPU:33, one launch (start us, length us, event | category | flops | bytes accessed | tf_op | source)
XLA Modules:
  0.0 134.1 jit_solution(2811934085107749783)
XLA Ops:
  0.6 1.0 copy.17
  1.6 0.6 copy-done.4
  2.3 0.1 multiply_convert_fusion.1
  2.4 0.8 copy-done.3
  3.2 0.1 copy.18
  3.4 0.0 copy-start
  3.4 0.1 pad_select_fusion.xs
  3.5 0.6 copy-done.5
  4.2 0.0 copy-done.6
  4.2 0.2 select_reduce_fusion.1
  4.4 0.1 fusion.3
  4.5 0.2 reduce_window_sum.11
  4.6 0.2 select_reduce_fusion
  4.9 0.2 fusion.2
  5.2 1.0 copy-done.1
  6.2 1.0 copy-done.2
  7.2 122.4 %expert_layer.1 = (bf16[256,512]{1,0:T(8,128)(2,1)S(1)}, f32[1792,128]{1,0:T(8,128)S(1)}, f32[1792,128]{1,0:T(8,128)S(1)}, f32[128,1792]{1,0:T(8,128)S(1)}) custom-call(bf16[256,512]{1,0:T(8,128)(2,1)S(1)} %pad_select_fusion.xs, bf16[256,256]{1,0:T(8,128)(2,1)S(1)} %copy_bitcast_fusion.pp, bf16[1792,128]{1,0:T(8,128)(2,1)S(1)} %bitcast.16, ...), custom_call_target="tpu_custom_call" | custom-call | tf_op jit(solution)/shard_map/expert_layer/pallas_call | solution.py:351
  129.6 0.1 slice_select_fusion
  129.7 0.1 multiply_convert_fusion
  129.8 0.8 copy.20
  130.6 0.8 copy.21
  131.3 0.9 copy.27
  132.3 0.9 copy.28
  133.2 0.9 copy.29
  (12 shorter events, 0.1 us)
Async XLA Ops:
  1.6 0.7 copy-start.4
  2.3 0.9 copy-start.3
  3.4 1.8 %copy-start = (bf16[1,1792,128]{2,1,0:T(8,128)(2,1)S(1)}, bf16[1,1792,128]{2,1,0:T(8,128)(2,1)}, u32[]{:S(2)}) copy-start(bf16[1,1792,128]{2,1,0:T(8,128)(2,1)} %param.12) | copy-start | bytes 1376260
  3.5 0.7 copy-start.5
  3.5 0.7 copy-start.6
  5.1 1.0 copy-start.1
  6.2 1.0 copy-start.2

commit v2 on v1

v2 whole, which is shorter than its diff:
```python
import jax
import jax.numpy as jnp
from jax import lax
from jax.experimental import pallas as pl
from jax.experimental.pallas import tpu as pltpu
from jax.sharding import PartitionSpec as P

CHUNKS = 8
LAGS = (0, 3, 4, 5, 6, 8, 11, 12, 13, 14)
WIDE = 896
HALF = 448
KERNEL_VMEM = 60 * 2**20
F32 = jnp.float32
BF16 = jnp.bfloat16


def base_offset(chunk):
    half = chunk // 2
    odd = jnp.where(chunk == 1, 4, 8 - half)
    return jnp.where(chunk % 2 == 0, half, odd)


def place():
    a, e, s = lax.axis_index("attn"), lax.axis_index("exp"), lax.axis_index("shard")
    return a % 4, a // 4 + 8 * s, e // 2, e % 2, s


def device(y, z, x, c):
    return {"attn": (z % 8) * 4 + y, "exp": 2 * x + c, "shard": z // 8}


def send(src, dst, send_sem, recv_sem, target):
    return pltpu.make_async_remote_copy(
        src_ref=src,
        dst_ref=dst,
        send_sem=send_sem,
        recv_sem=recv_sem,
        device_id=target,
        device_id_type=pl.DeviceIdType.MESH,
    )


def wait_for(ref, sem):
    pltpu.make_async_copy(ref, ref, sem).wait()


def last_last(a, b):
    return lax.dot_general(a, b, (((1,), (1,)), ((), ())), preferred_element_type=F32)


def first_first(a, b):
    return lax.dot_general(a, b, (((0,), (0,)), ((), ())), preferred_element_type=F32)


def dot(a, b):
    return jnp.dot(a, b, preferred_element_type=F32)


def kernel(
    tokens_far, cot_far, ids_far, gates_far, table_far, wg, wu, wd_far,
    mixed_far, back_far, gg_far, gu_far, gd_far, mixed, back, gg, gu, gd, g_s, tokens, cotangent, ids, gates, table, tok, ex, pp, sb, rows, wgu, wd, acc, es, em, er, lg, os, orr, cs, fr, xr, rb, rr, tb, tr,
    i_r, w_r, tok_s, tok_r, d_s, d_r, ag_s, ag_r, sf_s, sf_r, e_s, e_r, o_s, o_r, x_s, x_r, b_s, b_r, t_s, t_r,
):
    y, z, x, c, s = place()
    other = 3 - x
    p_own = jnp.where(x // 2 == s, 0, 1)
    qi_own = jnp.where(p_own == 0, x, other) - 2 * s
    h_src = jnp.where(c == 0, x, other) // 2
    h_fin = x // 2
    x_fin = jnp.where(p_own == 0, x, other)
    has_self = (c == 0) & (p_own == 0)
    sibling = device(y, z, x, 1 - c)
    z_up, z_dn = device(y, (z + 4) % 16, x, c), device(y, (z + 12) % 16, x, c)

    def piece_of(xx):
        p = jnp.where(xx // 2 == s, 0, 1)
        return jnp.where(p == 0, xx, 3 - xx) - 2 * s, p

    loads = []
    for i, (far, near) in enumerate(
        ((tokens_far, tokens), (cot_far, cotangent), (ids_far, ids), (gates_far, gates), (table_far, table))
    ):
        loads.append(pltpu.make_async_copy(far, near, i_r.at[i]))
        loads[-1].start()

    barrier = pltpu.get_barrier_semaphore()

    def greet(target):
        pl.semaphore_signal(barrier, inc=1, device_id=target, device_id_type=pl.DeviceIdType.MESH)

    greet(sibling)
    greet(z_up)
    greet(z_dn)
    for r in (1, 3):
        greet(device(y, z, (x + r) % 4, c))

    @pl.when(c == 0)
    def _():
        greet(device(y, z, x, 1))

    @pl.when(c == 1)
    def _():
        greet(device(y, z, other, 0))
        greet(device(y, z, other, 1))

    def greet_sources(i, carry):
        @pl.when(jnp.logical_not(has_self & (i == 0)))
        def _():
            greet(device((y + p_own + 2 * c) % 4, (z + i) % 16, x, p_own))

        return carry

    lax.fori_loop(0, 16, greet_sources, 0)
    x_back = jnp.where(c == 0, x, other)

    def greet_owners(i, carry):
        c_r = i % 2
        zz = 8 * h_fin + i // 2

        @pl.when(jnp.logical_not(has_self & (c_r == 0) & (zz == z)))
        def _():
            greet(device((y + 8 - c - 2 * c_r) % 4, zz, x_back, c_r))

        return carry

    lax.fori_loop(0, 16, greet_owners, 0)

    weights = [pltpu.make_async_copy(wd_far.at[0], wd, w_r.at[0])]
    for q in range(2):
        half = pl.ds(q * WIDE, WIDE)
        weights.append(pltpu.make_async_copy(wg.at[0, half], wgu.at[q, :, pl.ds(0, 128)], w_r.at[1 + q]))
        weights.append(pltpu.make_async_copy(wu.at[0, half], wgu.at[q, :, pl.ds(128, 128)], w_r.at[3 + q]))
    for load in weights:
        load.start()
    for load in loads:
        load.wait()

    tok[:, 0:128] = tokens[...]
    tok[:, 128:256] = (gates[...] * cotangent[...].astype(F32)).astype(BF16)

    pl.semaphore_wait(barrier, 6 + c + 32 - 2 * has_self.astype(jnp.int32))

    across = device(y, z, other, 1)

    @pl.when(c == 0)
    def _():
        send(tok, ex.at[0], tok_s.at[0], tok_r.at[0], across).start()

    @pl.when(c == 1)
    def _():
        send(tok, ex.at[1], tok_s.at[1], tok_r.at[1], device(y, z, x, 0)).start()
        send(tok, ex.at[1], tok_s.at[0], tok_r.at[1], across).start()

    row32 = lax.broadcasted_iota(jnp.int32, (32, 128), 0)
    named = (jnp.broadcast_to(ids[...], (32, 128)) == row32).astype(BF16)
    renamed = jnp.broadcast_to(table[...], (32, 32)) == lax.broadcasted_iota(jnp.int32, (32, 32), 0)
    member = dot(renamed.astype(BF16), named)
    earlier = lax.broadcasted_iota(jnp.int32, (128, 128), 0) < lax.broadcasted_iota(
        jnp.int32, (128, 128), 1
    )
    before = dot(member.astype(BF16), earlier.astype(BF16))
    rank_of = jnp.sum(member * before, axis=0, keepdims=True).astype(jnp.int32)
    slot_of = jnp.sum(member * row32.astype(F32), axis=0, keepdims=True).astype(jnp.int32)
    index = lax.broadcasted_iota(jnp.int32, (256, 128), 0)
    block, kind, rank = index // 16, (index // 8) % 2, index % 8
    offset = base_offset(block // 2)
    slot = ((z + 16 - offset) % 8) * 4 + (y + 8 - c - 2 * (block % 2)) % 4
    hit = (slot == slot_of) & (rank == rank_of)
    pp[:, 0:128] = (hit & (kind == 0)).astype(BF16)
    pp[:, 128:256] = (hit & (kind == 1)).astype(BF16)

    @pl.when(c == 0)
    def _():
        ex[0] = tok[...]

    @pl.when(c == 1)
    def _():
        wait_for(ex.at[0], tok_r.at[0])

    wait_for(ex.at[1], tok_r.at[1])
    sb[...] = last_last(pp[...], ex[...].reshape(WIDE, 256)).astype(BF16).reshape(16, 16, WIDE)

    def dispatch(i, carry):
        k, c_r = i // 2, i % 2
        zd = (z + 16 - base_offset(k)) % 16
        hi = jnp.where(zd // 8 == h_src, 0, 1)
        target = device((y + 8 - c - 2 * c_r) % 4, 8 * h_src + zd % 8, x, c_r)
        q_t = jnp.where(c == 0, x, other)
        there = rows.at[q_t - 2 * h_src, k, c_r, c, hi]
        mine = has_self & (i == 0)

        @pl.when(mine)
        def _():
            pltpu.make_async_copy(sb.at[i], there, d_r.at[k]).start()

        @pl.when(jnp.logical_not(mine))
        def _():
            send(sb.at[i], there, d_s.at[jnp.where(i == 0, CHUNKS, k)], d_r.at[k], target).start()

        return carry

    def give_out(k):
        lax.fori_loop(2 * k, 2 * k + 2, dispatch, 0)

    up, down_x = device(y, z, (x + 1) % 4, c), device(y, z, (x + 3) % 4, c)
    qi_up, p_up = piece_of((x + 1) % 4)
    qi_dn, p_dn = piece_of((x + 3) % 4)
    qi_far, p_far = piece_of((x + 2) % 4)
    low, high = pl.ds(0, 1), pl.ds(1, 1)
    first, second = pl.ds(0, 32), pl.ds(32, 32)

    def gather(k):
        own = rows.at[qi_own, k, c, p_own]
        wait_for(own, d_r.at[k])
        send(own, own, ag_s.at[k, 0], ag_r.at[k, 0], up).start()
        send(own, own, ag_s.at[k, 1], ag_r.at[k, 1], down_x).start()

    def relay(k):
        wait_for(rows.at[qi_dn, k, c, p_dn], ag_r.at[k, 0])
        part = rows.at[qi_dn, k, c, p_dn, low]
        send(part, part, ag_s.at[k, 2], ag_r.at[k, 2], up).start()
        wait_for(rows.at[qi_up, k, c, p_up], ag_r.at[k, 1])
        part = rows.at[qi_up, k, c, p_up, high]
        send(part, part, ag_s.at[k, 3], ag_r.at[k, 3], down_x).start()

    def forward(k):
        wait_for(rows.at[qi_far, k, c, p_far, low], ag_r.at[k, 2])
        wait_for(rows.at[qi_far, k, c, p_far, high], ag_r.at[k, 3])
        for q in range(2):
            send(rows.at[q, k, c], rows.at[q, k, c], sf_s.at[k, q], sf_r.at[k, q], sibling).start()

    def project(k):
        for q in range(2):
            wait_for(rows.at[q, k, 1 - c], sf_r.at[k, q])
        both = jnp.zeros((128, 256), F32)
        down = jnp.zeros((128, 128), F32)
        for q in range(2):
            block = rows[q, k].reshape(128, WIDE)
            both = both + dot(block, wgu[q])
            down = down + last_last(block, wd[:, q * WIDE : (q + 1) * WIDE])
        part = jnp.concatenate(
            [both.reshape(8, 2, 8, 256)[:, 0], down.reshape(8, 2, 8, 128)[:, 1]], axis=-1
        )
        acc[k] = part.reshape(64, 384)
        pairs = part.reshape(4, 2, 8, 384)
        es[k] = jnp.concatenate([pairs[:, 1:], pairs[:, :1]], axis=1).reshape(64, 384).astype(BF16)
        send(es.at[k, first], em.at[k, first], e_s.at[k, 0], e_r.at[k, 0], z_up).start()
        send(es.at[k, second], em.at[k, second], e_s.at[k, 1], e_r.at[k, 1], z_dn).start()

    def hop(k):
        wait_for(em.at[k, first], e_r.at[k, 0])
        send(em.at[k, first], er.at[k, first], e_s.at[k, 2], e_r.at[k, 2], z_up).start()
        wait_for(em.at[k, second], e_r.at[k, 1])
        send(em.at[k, second], er.at[k, second], e_s.at[k, 3], e_r.at[k, 3], z_dn).start()

    def expand(k):
        wait_for(er.at[k, first], e_r.at[k, 2])
        wait_for(er.at[k, second], e_r.at[k, 3])
        total = acc[k] + er[k].astype(F32)
        gate, up, d_hid = total[:, :128], total[:, 128:256], total[:, 256:]
        sigma = jax.nn.sigmoid(gate)
        hidden = gate * sigma * up
        d_gate = d_hid * up * sigma * (1.0 + gate * (1.0 - sigma))
        d_up = d_hid * gate * sigma
        d_both = jnp.concatenate([d_gate, d_up], axis=1)
        nothing = jnp.zeros((8, 8, 128), F32)
        over = jnp.concatenate([d_both.reshape(8, 8, 256), nothing], axis=-1)
        under = jnp.concatenate([nothing, nothing, hidden.reshape(8, 8, 128)], axis=-1)
        lg[k] = jnp.stack([over, under], axis=1).reshape(128, 384).astype(BF16)
        hidden, d_both = hidden.astype(BF16), d_both.astype(BF16)
        for q in range(2):
            outs = dot(hidden, wd[:, q * WIDE : (q + 1) * WIDE]).reshape(8, 8, WIDE)
            ins = last_last(d_both, wgu[q]).reshape(8, 8, WIDE)
            shares = jnp.stack([outs, ins], axis=1).reshape(2, 2, 2, 16, WIDE).astype(BF16)
            os[k, 0, q] = shares[0]
            os[k, 1, q] = shares[1]
        send(os.at[k, 1 - c], orr.at[k], o_s.at[k], o_r.at[k], sibling).start()

    def scatter(k):
        wait_for(orr.at[k], o_r.at[k])
        for q in range(2):
            cs[k, q] = (os[k, c, q].astype(F32) + orr[k, q].astype(F32)).astype(BF16)
        send(cs.at[k, qi_far, p_far, low], fr.at[k, 0], x_s.at[k, 0], x_r.at[k, 0], up).start()
        send(cs.at[k, qi_far, p_far, high], fr.at[k, 1], x_s.at[k, 1], x_r.at[k, 1], down_x).start()

    def combine(k):
        wait_for(fr.at[k, 0], x_r.at[k, 0])
        cs[k, qi_up, p_up, 0:1] = (cs[k, qi_up, p_up, 0:1].astype(F32) + fr[k, 0].astype(F32)).astype(BF16)
        send(cs.at[k, qi_up, p_up], xr.at[k, 0], x_s.at[k, 2], x_r.at[k, 2], up).start()
        wait_for(fr.at[k, 1], x_r.at[k, 1])
        cs[k, qi_dn, p_dn, 1:2] = (cs[k, qi_dn, p_dn, 1:2].astype(F32) + fr[k, 1].astype(F32)).astype(BF16)
        send(cs.at[k, qi_dn, p_dn], xr.at[k, 1], x_s.at[k, 3], x_r.at[k, 3], down_x).start()

    def give_back(k):
        total = cs[k, qi_own, p_own].astype(F32)
        for r in range(2):
            wait_for(xr.at[k, r], x_r.at[k, 2 + r])
            total = total + xr[k, r].astype(F32)
        rb[k] = total.astype(BF16)
        there = rr.at[2 * k + c]
        for hi in range(2):
            zs = (z + base_offset(k) + 8 * hi) % 16
            target = device((y + p_own + 2 * c) % 4, zs, x_fin, p_own)
            go = send(rb.at[k, hi], there, b_s.at[k, hi], b_r.at[k], target)
            if hi == 0:
                mine = has_self & (k == 0)

                @pl.when(mine)
                def _():
                    pltpu.make_async_copy(rb.at[k, 0], there, b_r.at[k]).start()

                @pl.when(jnp.logical_not(mine))
                def _():
                    go.start()

            else:
                go.start()

    order = (give_out, gather, relay, forward, project, hop, expand, scatter, combine, give_back)
    stages = tuple(zip(order, LAGS))

    def step(t, carry):
        for stage, lag in stages:

            @pl.when((t >= lag) & (t < lag + CHUNKS))
            def _():
                stage(t - lag)

        return carry

    for load in weights:
        load.wait()
    lax.fori_loop(0, CHUNKS + LAGS[-1], step, 0)

    factors = lg[...].reshape(1024, 384).T
    for q in range(2):

        def columns(n, carry):
            lanes = pl.ds(pl.multiple_of(n * 128, 128), 128)
            block = rows[q, :, :, :, :, :, lanes].reshape(1024, 128)
            grads = dot(factors, block)
            at = pl.ds(pl.multiple_of(q * WIDE + n * 128, 128), 128)
            gg[at, :] = grads[:128].T
            gu[at, :] = grads[128:256].T
            gd[:, at] = grads[256:]
            return carry

        lax.fori_loop(0, 7, columns, 0)

    stores = [
        pltpu.make_async_copy(near, far, g_s.at[i])
        for i, (near, far) in enumerate(
            ((mixed, mixed_far), (back, back_far), (gg, gg_far), (gu, gu_far), (gd, gd_far))
        )
    ]
    for copy in stores[2:]:
        copy.start()
    for k in range(CHUNKS):
        wait_for(rr.at[pl.ds(2 * k, 2)], b_r.at[k])
    tb[...] = first_first(rr[...].reshape(256, WIDE), pp[...]).astype(BF16).reshape(2, HALF, 256)
    swap = send(tb.at[1 - c], tr, t_s, t_r, sibling)
    swap.start()

    wait_for(tok, tok_s.at[0])

    @pl.when(c == 1)
    def _():
        wait_for(tok, tok_s.at[1])

    wait_for(sb.at[1], d_s.at[0])
    for k in range(1, CHUNKS):
        wait_for(sb.at[pl.ds(2 * k, 2)], d_s.at[k])

    @pl.when(jnp.logical_not(has_self))
    def _():
        wait_for(sb.at[0], d_s.at[CHUNKS])
        wait_for(rb.at[0, 0], b_s.at[0, 0])

    def drain(k, carry):
        for r in range(2):
            wait_for(xr.at[k, r], ag_s.at[k, r])
            wait_for(fr.at[k, r], ag_s.at[k, 2 + r])
            wait_for(fr.at[k, r], x_s.at[k, r])
            wait_for(xr.at[k, r], x_s.at[k, 2 + r])
        for q in range(2):
            wait_for(rows.at[q, k, c], sf_s.at[k, q])
        wait_for(es.at[k, first], e_s.at[k, 0])
        wait_for(es.at[k, second], e_s.at[k, 1])
        wait_for(em.at[k, first], e_s.at[k, 2])
        wait_for(em.at[k, second], e_s.at[k, 3])
        wait_for(orr.at[k], o_s.at[k])
        for i in range(2):
            if i == 0:

                @pl.when(k > 0)
                def _():
                    wait_for(rb.at[k, 0], b_s.at[k, 0])

            else:
                wait_for(rb.at[k, i], b_s.at[k, i])
        return carry

    lax.fori_loop(0, CHUNKS, drain, 0)
    swap.wait()
    mixed[...] = (gates[...] * (tb[c, :, 0:128] + tr[:, 0:128]).astype(F32)).astype(BF16)
    stores[0].start()
    back[...] = tb[c, :, 128:256] + tr[:, 128:256]
    stores[1].start()
    for copy in stores:
        copy.wait()


def store(*refs):
    far, out, near, sems = refs[0:5], refs[5:10], refs[10:15], refs[15]
    order = (2, 3, 4, 0, 1)
    for i in order:
        pltpu.make_async_copy(far[i], near[i], sems.at[0, i]).start()
    for i in order:
        pltpu.make_async_copy(far[i], near[i], sems.at[0, i]).wait()
        pltpu.make_async_copy(near[i], out[i], sems.at[1, i]).start()
    for i in order:
        pltpu.make_async_copy(near[i], out[i], sems.at[1, i]).wait()


def shards(tokens, route_ids, gate_values, slot_table, w_gate, w_up, w_down, cotangent):
    hbm = pl.BlockSpec(memory_space=pltpu.HBM)
    sem = pltpu.SemaphoreType.DMA
    shapes = (
        jax.ShapeDtypeStruct((HALF, 128), BF16),
        jax.ShapeDtypeStruct((HALF, 128), BF16),
        jax.ShapeDtypeStruct((1792, 128), F32),
        jax.ShapeDtypeStruct((1792, 128), F32),
        jax.ShapeDtypeStruct((128, 1792), F32),
    )
    results = pl.pallas_call(
        kernel,
        name="expert_layer",
        out_shape=shapes,
        in_specs=[hbm] * 8,
        out_specs=(hbm,) * 5,
        scratch_shapes=[
            pltpu.VMEM((HALF, 128), BF16),
            pltpu.VMEM((HALF, 128), BF16),
            pltpu.VMEM((1792, 128), F32),
            pltpu.VMEM((1792, 128), F32),
            pltpu.VMEM((128, 1792), F32),
            sem((5,)),
            pltpu.VMEM((HALF, 128), BF16),
            pltpu.VMEM((HALF, 128), BF16),
            pltpu.VMEM((1, 128), jnp.int32),
            pltpu.VMEM((1, 128), F32),
            pltpu.VMEM((1, 32), jnp.int32),
            pltpu.VMEM((HALF, 256), BF16),
            pltpu.VMEM((2, HALF, 256), BF16),
            pltpu.VMEM((256, 256), BF16),
            pltpu.VMEM((16, 16, WIDE), BF16),
            pltpu.VMEM((2, CHUNKS, 2, 2, 2, 16, WIDE), BF16),
            pltpu.VMEM((2, WIDE, 256), BF16),
            pltpu.VMEM((128, 1792), BF16),
            pltpu.VMEM((CHUNKS, 64, 384), F32),
            pltpu.VMEM((CHUNKS, 64, 384), BF16),
            pltpu.VMEM((CHUNKS, 64, 384), BF16),
            pltpu.VMEM((CHUNKS, 64, 384), BF16),
            pltpu.VMEM((CHUNKS, 128, 384), BF16),
            pltpu.VMEM((CHUNKS, 2, 2, 2, 2, 16, WIDE), BF16),
            pltpu.VMEM((CHUNKS, 2, 2, 2, 16, WIDE), BF16),
            pltpu.VMEM((CHUNKS, 2, 2, 2, 16, WIDE), BF16),
            pltpu.VMEM((CHUNKS, 2, 1, 16, WIDE), BF16),
            pltpu.VMEM((CHUNKS, 2, 2, 16, WIDE), BF16),
            pltpu.VMEM((CHUNKS, 2, 16, WIDE), BF16),
            pltpu.VMEM((16, 16, WIDE), BF16),
            pltpu.VMEM((2, HALF, 256), BF16),
            pltpu.VMEM((HALF, 256), BF16),
            sem((5,)),
            sem((5,)),
            sem((2,)),
            sem((2,)),
            sem((CHUNKS + 1,)),
            sem((CHUNKS,)),
            sem((CHUNKS, 4)),
            sem((CHUNKS, 4)),
            sem((CHUNKS, 2)),
            sem((CHUNKS, 2)),
            sem((CHUNKS, 4)),
            sem((CHUNKS, 4)),
            sem((CHUNKS,)),
            sem((CHUNKS,)),
            sem((CHUNKS, 4)),
            sem((CHUNKS, 4)),
            sem((CHUNKS, 4)),
            sem((CHUNKS,)),
            sem,
            sem,
        ],
        compiler_params=pltpu.CompilerParams(
            collective_id=0, has_side_effects=True, vmem_limit_bytes=KERNEL_VMEM
        ),
    )(
        tokens.T,
        cotangent.T,
        route_ids.reshape(1, 128),
        gate_values.reshape(1, 128),
        slot_table.reshape(1, 32),
        w_gate,
        w_up,
        w_down,
    )
    mixed, back, grad_gate, grad_up, grad_down = pl.pallas_call(
        store,
        name="store",
        out_shape=shapes,
        in_specs=[hbm] * 5,
        out_specs=(hbm,) * 5,
        scratch_shapes=[pltpu.VMEM(shape.shape, shape.dtype) for shape in shapes] + [sem((2, 5))],
        compiler_params=pltpu.CompilerParams(vmem_limit_bytes=KERNEL_VMEM),
    )(*results)
    return mixed.T, back.T, grad_gate[None], grad_up[None], grad_down[None]


def solution(mesh):
    in_specs = (
        P(("attn", "shard"), "exp"),
        P(("attn", "shard"), None),
        P(("attn", "shard"), None),
        P(),
        P("attn", "shard", "exp"),
        P("attn", "shard", "exp"),
        P("attn", "exp", "shard"),
        P(("attn", "shard"), "exp"),
    )
    out_specs = (
        P(("attn", "shard"), "exp"),
        P(("attn", "shard"), "exp"),
        P("attn", "shard", "exp"),
        P("attn", "shard", "exp"),
        P("attn", "exp", "shard"),
    )
    return jax.shard_map(shards, mesh=mesh, in_specs=in_specs, out_specs=out_specs, check_vma=False)
```

time: 134 us -> 124 us (0.925)
  the two profiles are of different devices: /device:TPU:33 before, /device:TPU:101 now
where the time goes in v2:
time: 124 us
  Pallas kernels  123 us (99%)
    pallas_call x1, Pallas kernels, shards(): pl.pallas_call(kernel, name='expert_layer', out_shape=shapes, in_specs=[h...  120 us
    pallas_call x1, Pallas kernels, shards(): pl.pallas_call(store, name='store', out_shape=shapes, in_specs=[hbm] * 5,...  2.86 us

profile of v2, /device:TPU:101, one launch (start us, length us, event | category | flops | bytes accessed | tf_op | source)
XLA Modules:
  0.0 124.0 jit_solution(11050746414997714654)
XLA Ops:
  0.6 120.5 %expert_layer.1 = (bf16[448,128]{1,0:T(8,128)(2,1)}, bf16[448,128]{1,0:T(8,128)(2,1)}, f32[1792,128]{1,0:T(8,128)}, f32[1792,128]{1,0:T(8,128)}, f32[128,1792]{1,0:T(8,128)}) custom-call(bf16[448,128]{1,0:T(8,128)(2,1)} %bitcast.10, bf16[448,128]{1,0:T(8,128)(2,1)} %bitcast.11, s32[1,128]{1,0:T(1,128)} %bitcast.12, f32[1,128]{1,0:T(1,128)} %bitcast.13, ...), custom_call_target="tpu_custom_call" | custom-call | tf_op jit(solution)/shard_map/expert_layer/pallas_call | solution.py:435
  121.1 2.9 %store.1 = (bf16[448,128]{1,0:T(8,128)(2,1)}, bf16[448,128]{1,0:T(8,128)(2,1)}, f32[1792,128]{1,0:T(8,128)}, f32[1792,128]{1,0:T(8,128)}, f32[128,1792]{1,0:T(8,128)}) custom-call(bf16[448,128]{1,0:T(8,128)(2,1)} %get-tuple-element.15.refs_0_, bf16[448,128]{1,0:T(8,128)(2,1)} %get-tuple-element.16.refs_1_, f32[1792,128]{1,0:T(8,128)} %get-tuple-element.17.refs_2_, ...), custom_call_target="tpu_custom_call" | custom-call | tf_op jit(solution)/shard_map/store/pallas_call | solution.py:508

commit v3 on v2

--- a/solution.py
+++ b/solution.py
@@ -6,7 +6,7 @@
 from jax.sharding import PartitionSpec as P
 
 CHUNKS = 8
-LAGS = (0, 3, 4, 5, 6, 8, 11, 12, 13, 14)
+LAGS = (0, 3, 4, 5, 7, 10, 11, 12)
 WIDE = 896
 HALF = 448
 KERNEL_VMEM = 60 * 2**20
@@ -58,7 +58,7 @@
 
 def kernel(
     tokens_far, cot_far, ids_far, gates_far, table_far, wg, wu, wd_far,
-    mixed_far, back_far, gg_far, gu_far, gd_far, mixed, back, gg, gu, gd, g_s, tokens, cotangent, ids, gates, table, tok, ex, pp, sb, rows, wgu, wd, acc, es, em, er, lg, os, orr, cs, fr, xr, rb, rr, tb, tr,
+    mixed_far, back_far, gg_far, gu_far, gd_far, mixed, back, gg, gu, gd, g_s, tokens, cotangent, ids, gates, table, tok, ex, pp, sb, rows, wgu, wd, acc, es, em, er, lg, os, orr, cs, xr, rb, rr, tb, tr,
     i_r, w_r, tok_s, tok_r, d_s, d_r, ag_s, ag_r, sf_s, sf_r, e_s, e_r, o_s, o_r, x_s, x_r, b_s, b_r, t_s, t_r,
 ):
     y, z, x, c, s = place()
@@ -91,7 +91,7 @@
     greet(sibling)
     greet(z_up)
     greet(z_dn)
-    for r in (1, 3):
+    for r in (1, 2, 3):
         greet(device(y, z, (x + r) % 4, c))
 
     @pl.when(c == 0)
@@ -138,7 +138,7 @@
     tok[:, 0:128] = tokens[...]
     tok[:, 128:256] = (gates[...] * cotangent[...].astype(F32)).astype(BF16)
 
-    pl.semaphore_wait(barrier, 6 + c + 32 - 2 * has_self.astype(jnp.int32))
+    pl.semaphore_wait(barrier, 7 + c + 32 - 2 * has_self.astype(jnp.int32))
 
     across = device(y, z, other, 1)
 
@@ -202,30 +202,21 @@
     def give_out(k):
         lax.fori_loop(2 * k, 2 * k + 2, dispatch, 0)
 
-    up, down_x = device(y, z, (x + 1) % 4, c), device(y, z, (x + 3) % 4, c)
     qi_up, p_up = piece_of((x + 1) % 4)
     qi_dn, p_dn = piece_of((x + 3) % 4)
     qi_far, p_far = piece_of((x + 2) % 4)
-    low, high = pl.ds(0, 1), pl.ds(1, 1)
     first, second = pl.ds(0, 32), pl.ds(32, 32)
 
     def gather(k):
         own = rows.at[qi_own, k, c, p_own]
         wait_for(own, d_r.at[k])
-        send(own, own, ag_s.at[k, 0], ag_r.at[k, 0], up).start()
-        send(own, own, ag_s.at[k, 1], ag_r.at[k, 1], down_x).start()
-
-    def relay(k):
+        for r in (1, 2, 3):
+            send(own, own, ag_s.at[k, r - 1], ag_r.at[k, r - 1], device(y, z, (x + r) % 4, c)).start()
+
+    def forward(k):
         wait_for(rows.at[qi_dn, k, c, p_dn], ag_r.at[k, 0])
-        part = rows.at[qi_dn, k, c, p_dn, low]
-        send(part, part, ag_s.at[k, 2], ag_r.at[k, 2], up).start()
-        wait_for(rows.at[qi_up, k, c, p_up], ag_r.at[k, 1])
-        part = rows.at[qi_up, k, c, p_up, high]
-        send(part, part, ag_s.at[k, 3], ag_r.at[k, 3], down_x).start()
-
-    def forward(k):
-        wait_for(rows.at[qi_far, k, c, p_far, low], ag_r.at[k, 2])
-        wait_for(rows.at[qi_far, k, c, p_far, high], ag_r.at[k, 3])
+        wait_for(rows.at[qi_far, k, c, p_far], ag_r.at[k, 1])
+        wait_for(rows.at[qi_up, k, c, p_up], ag_r.at[k, 2])
         for q in range(2):
             send(rows.at[q, k, c], rows.at[q, k, c], sf_s.at[k, q], sf_r.at[k, q], sibling).start()
 
@@ -280,21 +271,14 @@
         wait_for(orr.at[k], o_r.at[k])
         for q in range(2):
             cs[k, q] = (os[k, c, q].astype(F32) + orr[k, q].astype(F32)).astype(BF16)
-        send(cs.at[k, qi_far, p_far, low], fr.at[k, 0], x_s.at[k, 0], x_r.at[k, 0], up).start()
-        send(cs.at[k, qi_far, p_far, high], fr.at[k, 1], x_s.at[k, 1], x_r.at[k, 1], down_x).start()
-
-    def combine(k):
-        wait_for(fr.at[k, 0], x_r.at[k, 0])
-        cs[k, qi_up, p_up, 0:1] = (cs[k, qi_up, p_up, 0:1].astype(F32) + fr[k, 0].astype(F32)).astype(BF16)
-        send(cs.at[k, qi_up, p_up], xr.at[k, 0], x_s.at[k, 2], x_r.at[k, 2], up).start()
-        wait_for(fr.at[k, 1], x_r.at[k, 1])
-        cs[k, qi_dn, p_dn, 1:2] = (cs[k, qi_dn, p_dn, 1:2].astype(F32) + fr[k, 1].astype(F32)).astype(BF16)
-        send(cs.at[k, qi_dn, p_dn], xr.at[k, 1], x_s.at[k, 3], x_r.at[k, 3], down_x).start()
+        for r, (qi, p) in enumerate(((qi_up, p_up), (qi_far, p_far), (qi_dn, p_dn))):
+            there = device(y, z, (x + 1 + r) % 4, c)
+            send(cs.at[k, qi, p], xr.at[k, r], x_s.at[k, r], x_r.at[k, r], there).start()
 
     def give_back(k):
         total = cs[k, qi_own, p_own].astype(F32)
-        for r in range(2):
-            wait_for(xr.at[k, r], x_r.at[k, 2 + r])
+        for r in range(3):
+            wait_for(xr.at[k, r], x_r.at[k, r])
             total = total + xr[k, r].astype(F32)
         rb[k] = total.astype(BF16)
         there = rr.at[2 * k + c]
@@ -316,24 +300,11 @@
             else:
                 go.start()
 
-    order = (give_out, gather, relay, forward, project, hop, expand, scatter, combine, give_back)
+    order = (give_out, gather, forward, project, hop, expand, scatter, give_back)
     stages = tuple(zip(order, LAGS))
 
-    def step(t, carry):
-        for stage, lag in stages:
-
-            @pl.when((t >= lag) & (t < lag + CHUNKS))
-            def _():
-                stage(t - lag)
-
-        return carry
-
-    for load in weights:
-        load.wait()
-    lax.fori_loop(0, CHUNKS + LAGS[-1], step, 0)
-
-    factors = lg[...].reshape(1024, 384).T
-    for q in range(2):
+    def weight_gradients(q):
+        factors = lg[...].reshape(1024, 384).T
 
         def columns(n, carry):
             lanes = pl.ds(pl.multiple_of(n * 128, 128), 128)
@@ -347,6 +318,24 @@
 
         lax.fori_loop(0, 7, columns, 0)
 
+    def step(t, carry):
+        for stage, lag in stages:
+
+            @pl.when((t >= lag) & (t < lag + CHUNKS))
+            def _():
+                stage(t - lag)
+
+        @pl.when(t == CHUNKS + LAGS[-1] - 2)
+        def _():
+            weight_gradients(0)
+
+        return carry
+
+    for load in weights:
+        load.wait()
+    lax.fori_loop(0, CHUNKS + LAGS[-1], step, 0)
+
+    weight_gradients(1)
     stores = [
         pltpu.make_async_copy(near, far, g_s.at[i])
         for i, (near, far) in enumerate(
@@ -355,9 +344,12 @@
     ]
     for copy in stores[2:]:
         copy.start()
-    for k in range(CHUNKS):
+    for k in range(CHUNKS - 1):
         wait_for(rr.at[pl.ds(2 * k, 2)], b_r.at[k])
-    tb[...] = first_first(rr[...].reshape(256, WIDE), pp[...]).astype(BF16).reshape(2, HALF, 256)
+    early = first_first(rr[0:14].reshape(224, WIDE), pp[0:224])
+    wait_for(rr.at[pl.ds(14, 2)], b_r.at[CHUNKS - 1])
+    spread = early + first_first(rr[14:16].reshape(32, WIDE), pp[224:256])
+    tb[...] = spread.astype(BF16).reshape(2, HALF, 256)
     swap = send(tb.at[1 - c], tr, t_s, t_r, sibling)
     swap.start()
 
@@ -377,11 +369,9 @@
         wait_for(rb.at[0, 0], b_s.at[0, 0])
 
     def drain(k, carry):
-        for r in range(2):
+        for r in range(3):
+            wait_for(xr.at[k, r], x_s.at[k, r])
             wait_for(xr.at[k, r], ag_s.at[k, r])
-            wait_for(fr.at[k, r], ag_s.at[k, 2 + r])
-            wait_for(fr.at[k, r], x_s.at[k, r])
-            wait_for(xr.at[k, r], x_s.at[k, 2 + r])
         for q in range(2):
             wait_for(rows.at[q, k, c], sf_s.at[k, q])
         wait_for(es.at[k, first], e_s.at[k, 0])
@@ -412,14 +402,27 @@
 
 def store(*refs):
     far, out, near, sems = refs[0:5], refs[5:10], refs[10:15], refs[15]
-    order = (2, 3, 4, 0, 1)
-    for i in order:
-        pltpu.make_async_copy(far[i], near[i], sems.at[0, i]).start()
-    for i in order:
-        pltpu.make_async_copy(far[i], near[i], sems.at[0, i]).wait()
-        pltpu.make_async_copy(near[i], out[i], sems.at[1, i]).start()
-    for i in order:
-        pltpu.make_async_copy(near[i], out[i], sems.at[1, i]).wait()
+    parts = []
+    for i in (2, 3, 4, 0, 1):
+        rows = far[i].shape[0]
+        count = 4 if i > 1 else 1
+        for n in range(count):
+            parts.append((i, pl.ds(n * (rows // count), rows // count)))
+    reads = [
+        pltpu.make_async_copy(far[i].at[at], near[i].at[at], sems.at[0, n])
+        for n, (i, at) in enumerate(parts)
+    ]
+    writes = [
+        pltpu.make_async_copy(near[i].at[at], out[i].at[at], sems.at[1, n])
+        for n, (i, at) in enumerate(parts)
+    ]
+    for read in reads:
+        read.start()
+    for read, write in zip(reads, writes):
+        read.wait()
+        write.start()
+    for write in writes:
+        write.wait()
 
 
 def shards(tokens, route_ids, gate_values, slot_table, w_gate, w_up, w_down, cotangent):
@@ -465,8 +468,7 @@
             pltpu.VMEM((CHUNKS, 2, 2, 2, 2, 16, WIDE), BF16),
             pltpu.VMEM((CHUNKS, 2, 2, 2, 16, WIDE), BF16),
             pltpu.VMEM((CHUNKS, 2, 2, 2, 16, WIDE), BF16),
-            pltpu.VMEM((CHUNKS, 2, 1, 16, WIDE), BF16),
-            pltpu.VMEM((CHUNKS, 2, 2, 16, WIDE), BF16),
+            pltpu.VMEM((CHUNKS, 3, 2, 16, WIDE), BF16),
             pltpu.VMEM((CHUNKS, 2, 16, WIDE), BF16),
             pltpu.VMEM((16, 16, WIDE), BF16),
             pltpu.VMEM((2, HALF, 256), BF16),
@@ -485,8 +487,8 @@
             sem((CHUNKS, 4)),
             sem((CHUNKS,)),
             sem((CHUNKS,)),
-            sem((CHUNKS, 4)),
-            sem((CHUNKS, 4)),
+            sem((CHUNKS, 3)),
+            sem((CHUNKS, 3)),
             sem((CHUNKS, 4)),
             sem((CHUNKS,)),
             sem,
@@ -511,7 +513,7 @@
         out_shape=shapes,
         in_specs=[hbm] * 5,
         out_specs=(hbm,) * 5,
-        scratch_shapes=[pltpu.VMEM(shape.shape, shape.dtype) for shape in shapes] + [sem((2, 5))],
+        scratch_shapes=[pltpu.VMEM(shape.shape, shape.dtype) for shape in shapes] + [sem((2, 14))],
         compiler_params=pltpu.CompilerParams(vmem_limit_bytes=KERNEL_VMEM),
     )(*results)
     return mixed.T, back.T, grad_gate[None], grad_up[None], grad_down[None]

time: 124 us -> 123 us (level)
  the two profiles are of different devices: /device:TPU:101 before, /device:TPU:1 now
where the time goes in v3:
time: 123 us
  Pallas kernels  122 us (99%)
    pallas_call x1, Pallas kernels, shards(): pl.pallas_call(kernel, name='expert_layer', out_shape=shapes, in_specs=[h...  119 us
    pallas_call x1, Pallas kernels, shards(): pl.pallas_call(store, name='store', out_shape=shapes, in_specs=[hbm] * 5,...  2.96 us

profile of v3, /device:TPU:1, one launch (start us, length us, event | category | flops | bytes accessed | tf_op | source)
XLA Modules:
  0.0 123.0 jit_solution(10391487393763642914)
XLA Ops:
  0.6 119.4 %expert_layer.1 = (bf16[448,128]{1,0:T(8,128)(2,1)}, bf16[448,128]{1,0:T(8,128)(2,1)}, f32[1792,128]{1,0:T(8,128)}, f32[1792,128]{1,0:T(8,128)}, f32[128,1792]{1,0:T(8,128)}) custom-call(bf16[448,128]{1,0:T(8,128)(2,1)} %bitcast.10, bf16[448,128]{1,0:T(8,128)(2,1)} %bitcast.11, s32[1,128]{1,0:T(1,128)} %bitcast.12, f32[1,128]{1,0:T(1,128)} %bitcast.13, ...), custom_call_target="tpu_custom_call" | custom-call | tf_op jit(solution)/shard_map/expert_layer/pallas_call | solution.py:438
  120.1 3.0 %store.1 = (bf16[448,128]{1,0:T(8,128)(2,1)}, bf16[448,128]{1,0:T(8,128)(2,1)}, f32[1792,128]{1,0:T(8,128)}, f32[1792,128]{1,0:T(8,128)}, f32[128,1792]{1,0:T(8,128)}) custom-call(bf16[448,128]{1,0:T(8,128)(2,1)} %get-tuple-element.15.refs_0_, bf16[448,128]{1,0:T(8,128)(2,1)} %get-tuple-element.16.refs_1_, f32[1792,128]{1,0:T(8,128)} %get-tuple-element.17.refs_2_, ...), custom_call_target="tpu_custom_call" | custom-call | tf_op jit(solution)/shard_map/store/pallas_call | solution.py:510
